TPU v7x, 256 devices: a whole 4x4x8 slice. The times are simulated.
256 devices in a mesh: replica: 8 (over z_lo, x), tensor: 32 (over z_hi, y, core).
Axes of the slice: x: 4, y: 4, z: 8 (z_hi: 4, z_lo: 2; z = z_hi * 2 + z_lo), core: 2. Of those that a mesh axis runs over, the one named last changes fastest.
Arguments:
- tokens: bfloat16 [4096, 4096], P('replica', 'tensor'), may hold values from -6 to 6
- prev_gain: float32 [4096], replicated, may hold values from 0.1 to 1.9
- prev_gate_up: bfloat16 [4096, 2, 16384], P(None, None, 'tensor'), may hold values from -0.09375 to 0.09375
- prev_down: bfloat16 [16384, 4096], P('tensor', 'replica'), may hold values from -0.046875 to 0.046875
- next_gain: float32 [4096], replicated, may hold values from 0.1 to 1.9
- piece_buffer: bfloat16 [6144, 2, 16384], P('replica', None, 'tensor'), may hold values from -0.09375 to 0.09375
- slot_rows: int32 [6144], replicated, may hold values from 0 to 4096, as said below
- next_down: bfloat16 [16384, 4096], P('tensor', 'replica'), may hold values from -0.046875 to 0.046875
- score_head: float32 [4096, 2], P('tensor'), may hold values from -0.09375 to 0.09375
- step_positions: int32 [192], P('replica'), may hold values from 0 to 511, as said below
Outputs:
- layer_out: bfloat16 [4096, 4096], P('replica', 'tensor')
- step_logits: float32 [192, 2], P('replica')
Inputs may be any that keep to these rules, and one draw needn't show every extreme that they name: `slot_rows`: every row 0 to 4095 stands in exactly one slot. Slots r * 768 to (r + 1) * 768 - 1 belong to replica r; its filled slots come first, the rest hold 4096; some replica has all 768 slots filled. `step_positions`: within each replica's 24 entries the positions are distinct and rising; the first is 0 and the last is 511.
All inputs are finite; a program needn't handle non-finite values.
Results may differ from a plain program's by a relative error of at most 0.025.
Values may be sent and summed in bfloat16 or wider, within the bound.
A program may use at most 128 MiB of HBM per device.

v0:
```python
import jax
import jax.numpy as jnp
from jax import lax
from jax.sharding import PartitionSpec as P

D = 4096


def normalize(values, gain):
    floats = values.astype(jnp.float32)
    scale = lax.rsqrt(jnp.mean(floats * floats, axis=-1, keepdims=True) + 1e-06)
    return (floats * scale * gain).astype(jnp.bfloat16)


def activate(both, width):
    return (jax.nn.silu(both[:, :width]) * both[:, width:]).astype(jnp.bfloat16)


def shards(
    tokens,
    prev_gain,
    prev_gate_up,
    prev_down,
    next_gain,
    piece_buffer,
    slot_rows,
    next_down,
    score_head,
    step_positions,
):
    width = prev_down.shape[0]
    full_in = lax.all_gather(tokens, "tensor", axis=1, tiled=True)
    normed = normalize(full_in, prev_gain)
    both = jnp.dot(normed, prev_gate_up.reshape(D, 2 * width), preferred_element_type=jnp.float32)
    hidden = activate(both, width)
    partial_term = jnp.dot(
        hidden,
        lax.all_gather(prev_down, "replica", axis=1, tiled=True),
        preferred_element_type=jnp.float32,
    )
    share = lax.psum_scatter(
        partial_term.astype(jnp.bfloat16), "tensor", scatter_dimension=1, tiled=True
    ).astype(jnp.float32)
    middle = (tokens.astype(jnp.float32) + share).astype(jnp.bfloat16)
    full_mid = lax.all_gather(middle, "tensor", axis=1, tiled=True)
    normed_next = normalize(full_mid, next_gain)
    gathered = lax.all_gather(piece_buffer, "replica", axis=0, tiled=True)
    slot_count = slot_rows.shape[0]
    holder = (
        jnp.zeros((D + 1,), jnp.int32)
        .at[slot_rows]
        .set(jnp.arange(slot_count, dtype=jnp.int32))[:D]
    )
    flat_slots = gathered.reshape(slot_count, 2 * width)
    weights = jnp.take(flat_slots, holder, axis=0)
    both_next = jnp.dot(normed_next, weights, preferred_element_type=jnp.float32)
    hidden_next = activate(both_next, width)
    next_term = jnp.dot(
        hidden_next,
        lax.all_gather(next_down, "replica", axis=1, tiled=True),
        preferred_element_type=jnp.float32,
    )
    next_share = lax.psum_scatter(
        next_term.astype(jnp.bfloat16), "tensor", scatter_dimension=1, tiled=True
    ).astype(jnp.float32)
    layer_out = (middle.astype(jnp.float32) + next_share).astype(jnp.bfloat16)
    picked = jnp.take(layer_out, step_positions, axis=0).astype(jnp.float32)
    local_logits = jnp.dot(picked, score_head, precision=lax.Precision.HIGHEST)
    step_logits = lax.psum(local_logits, "tensor")
    return (layer_out, step_logits)


def solution(mesh):
    in_specs = (
        P("replica", "tensor"),
        P(),
        P(None, None, "tensor"),
        P("tensor", "replica"),
        P(),
        P("replica", None, "tensor"),
        P(),
        P("tensor", "replica"),
        P("tensor", None),
        P("replica"),
    )
    out_specs = (P("replica", "tensor"), P("replica", None))
    return jax.shard_map(shards, mesh=mesh, in_specs=in_specs, out_specs=out_specs, check_vma=False)
```

profile of v0, /device:TPU:2, one launch (start us, length us, event | category | flops | bytes accessed | tf_op | source)
XLA Modules:
  0.0 690.7 jit_solution(7837729822343438626)
XLA Ops:
  7.2 0.0 copy-start
  7.2 0.0 all-gather.6.cloned.1.call-start
  7.2 0.7 all-gather.6.cloned.1.call-update
  7.9 0.0 all-gather.8.cloned.1.call-start
  8.0 0.7 all-gather.8.cloned.1.call-update
  8.7 0.0 reduce-scatter.7.cloned.1.call-start
  8.7 0.0 copy-start.7
  8.7 9.3 %copy.16 = bf16[512,8,2,512]{3,1,2,0:T(8,128)(2,1)} copy(bf16[512,8,2,512]{3,2,1,0:T(2,128)(2,1)} %bitcast.16) | data formatting | bytes 16777216
  18.0 60.3 %all-gather.6.cloned.1.call-done = bf16[512,4096]{1,0:T(8,128)(2,1)} async-done(((bf16[512,128]{1,0:T(8,128)(2,1)}), bf16[512,4096]{1,0:T(8,128)(2,1)}) %all-gather.6.cloned.1.call-update) | async-done | bytes 4194320 | tf_op jit(solution)/shard_map/all_gather | solution.py:32
  78.4 3.2 fusion
  81.6 0.0 copy-done.7
  81.6 0.2 copy-done.2
  81.8 7.0 %fusion.10 = f32[512,1024]{1,0:T(8,128)S(1)} fusion(bf16[4096,1024]{1,0:T(8,128)(2,1)} %bitcast.17, bf16[512,4096]{1,0:T(8,128)(2,1)S(1)} %copy-done.2, f32[4096]{0:T(1024)S(1)} %copy-done.7, f32[512]{0:T(512)S(1)} %add_rsqrt_fusion.1), kind=kOutput, calls=%fused_computation.18 | convolution fusion | flops 4303355904 | bytes 14698496 | tf_op jit(solution)/shard_map/dot_general | solution.py:34
  88.8 41.6 %all-gather.8.cloned.1.call-done = bf16[512,4096]{1,0:T(8,128)(2,1)} async-done(((bf16[512,512]{1,0:T(8,128)(2,1)}), bf16[512,4096]{1,0:T(8,128)(2,1)}) %all-gather.8.cloned.1.call-update) | async-done | bytes 4194320 | tf_op jit(solution)/shard_map/all_gather | solution.py:38
  130.3 6.5 convolution_convert_fusion.1
  136.9 6.5 copy.12
  143.4 0.0 reduce-scatter.7.cloned.1.call-update
  143.4 0.0 all-gather.12.cloned.1.call-start
  143.4 0.5 all-gather.12.cloned.1.call-update
  144.0 0.0 all-gather.10.cloned.1.call-start
  144.0 100.3 %reduce-scatter.7.cloned.1.call-done = bf16[128,512]{1,0:T(8,128)(2,1)} async-done(((bf16[4096,512]{1,0:T(8,128)(2,1)}), bf16[128,512]{1,0:T(8,128)(2,1)}) %reduce-scatter.7.cloned.1.call-update) | async-done | bytes 131088
  244.3 1.0 copy.13
  245.4 0.0 copy-done.4
  245.4 0.7 add_convert_fusion.1
  246.1 0.0 all-gather.10.cloned.1.call-update
  246.1 0.0 all-gather.14.cloned.1.call-start
  246.1 0.5 all-gather.14.cloned.1.call-update
  246.7 0.0 reduce-scatter.9.cloned.1.call-start
  246.7 0.0 copy-done.6
  246.7 23.2 %scatter_custom_fusion = s32[4097]{0:T(1024)S(1)} fusion(s32[6144]{0:T(1024)S(1)} %compare_select_fusion, s32[6144]{0:T(1024)S(1)} %iota.3, s32[]{:T(128)} %constant.39.clone.1), kind=kCustom, calls=%fused_computation.36 | custom fusion | bytes 16392 | tf_op jit(solution)/shard_map/scatter | solution.py:52
  270.0 104.9 %all-gather.12.cloned.1.call-done = bf16[6144,2,512]{2,1,0:T(2,128)(2,1)} async-done(((bf16[768,2,512]{2,1,0:T(2,128)(2,1)}), bf16[6144,2,512]{2,1,0:T(2,128)(2,1)}) %all-gather.12.cloned.1.call-update) | async-done | bytes 12582928 | tf_op jit(solution)/shard_map/all_gather | solution.py:47
  374.9 12.6 %copy.17 = bf16[768,8,2,512]{3,1,2,0:T(8,128)(2,1)} copy(bf16[768,8,2,512]{3,2,1,0:T(2,128)(2,1)} %bitcast.15) | data formatting | bytes 25165824
  387.5 27.3 %gather_fusion = bf16[4096,1024]{1,0:T(8,128)(2,1)} fusion(bf16[6144,1024]{1,0:T(8,128)(2,1)} %bitcast.12, s32[4096]{0:T(1024)S(1)} %fusion.23), kind=kCustom, calls=%fused_computation | custom fusion | bytes 16793600 | tf_op jit(solution)/shard_map/jit(_take)/gather | solution.py:55
  414.8 29.2 %all-gather.10.cloned.1.call-done = bf16[512,4096]{1,0:T(8,128)(2,1)} async-done(((bf16[512,128]{1,0:T(8,128)(2,1)}), bf16[512,4096]{1,0:T(8,128)(2,1)}) %all-gather.10.cloned.1.call-update) | async-done | bytes 4194320 | tf_op jit(solution)/shard_map/all_gather | solution.py:45
  444.0 3.2 fusion.3
  447.3 0.2 copy-done.1
  447.5 8.0 %fusion.6 = f32[512,1024]{1,0:T(8,128)S(1)} fusion(bf16[4096,1024]{1,0:T(8,128)(2,1)} %gather_fusion, pred[4096]{0:T(1024)(128)(4,1)S(1)} %compare_and_fusion, bf16[512,4096]{1,0:T(8,128)(2,1)S(1)} %copy-done.1, f32[4096]{0:T(1024)S(1)} %copy-done.8, f32[512]{0:T(512)S(1)} %add_rsqrt_fusion), kind=kOutput, calls=%fused_computation.13 | convolution fusion | flops 4307550208 | bytes 14702592 | tf_op jit(solution)/shard_map/dot_general | solution.py:56
  455.5 40.5 %all-gather.14.cloned.1.call-done = bf16[512,4096]{1,0:T(8,128)(2,1)} async-done(((bf16[512,512]{1,0:T(8,128)(2,1)}), bf16[512,4096]{1,0:T(8,128)(2,1)}) %all-gather.14.cloned.1.call-update) | async-done | bytes 4194320 | tf_op jit(solution)/shard_map/all_gather | solution.py:60
  496.0 6.5 convolution_convert_fusion
  502.5 6.5 copy.14
  509.0 0.0 reduce-scatter.9.cloned.1.call-update
  509.0 0.6 copy-done.9
  509.7 100.3 %reduce-scatter.9.cloned.1.call-done = bf16[128,512]{1,0:T(8,128)(2,1)} async-done(((bf16[4096,512]{1,0:T(8,128)(2,1)}), bf16[128,512]{1,0:T(8,128)(2,1)}) %reduce-scatter.9.cloned.1.call-update) | async-done | bytes 131088
  609.9 1.0 copy.15
  611.0 0.0 copy-start.5
  611.0 0.6 gather_fusion.1
  611.6 0.2 fusion.26
  611.8 72.0 %psum.7 = f32[24,2]{0,1:T(2,128)} all-reduce(f32[24,2]{0,1:T(2,128)S(1)} %fusion.26), channel_id=1, replica_groups=mesh['replica'=8,'tensor'=32] {'tensor'}, use_global_device_ids=true, to_apply=%region_5.6 | all-reduce | flops 48 | bytes 384 | tf_op jit(solution)/shard_map/psum | solution.py:69
  (21 shorter events, 0.1 us)
Async XLA Ops:
  7.2 604.5 %copy-start = (f32[128,2]{0,1:T(2,128)S(1)}, f32[128,2]{0,1:T(2,128)}, u32[]{:S(2)}) copy-start(f32[128,2]{0,1:T(2,128)} %param.18) | copy-start | bytes 3076
  7.2 71.2 %all-gather.6.cloned.1.call-start = ((), (), s32[]{:S(2)}) async-start(), calls=%async_computation.2 | async-start | bytes 4325376 | tf_op jit(solution)/shard_map/all_gather | solution.py:32
  7.9 122.4 %all-gather.8.cloned.1.call-start = ((), (), s32[]{:S(2)}) async-start(), calls=%async_computation.3 | async-start | bytes 4718592 | tf_op jit(solution)/shard_map/all_gather | solution.py:38
  8.7 235.7 %reduce-scatter.7.cloned.1.call-start = ((), (), s32[]{:S(2)}) async-start(), calls=%async_computation.7 | async-start | bytes 4325376
  8.7 72.9 %copy-start.7 = (f32[4096]{0:T(1024)S(1)}, f32[4096]{0:T(1024)}, u32[]{:S(2)}) copy-start(f32[4096]{0:T(1024)} %param.11) | copy-start | bytes 49156
  78.4 3.4 copy-start.2
  143.4 102.0 %copy-start.4 = (bf16[512,128]{1,0:T(8,128)(2,1)S(1)}, bf16[512,128]{1,0:T(8,128)(2,1)}, u32[]{:S(2)}) copy-start(bf16[512,128]{1,0:T(8,128)(2,1)} %param.10) | copy-start | bytes 393220
  143.4 103.4 %copy-start.6 = (s32[6144]{0:T(1024)S(1)}, s32[6144]{0:T(1024)}, u32[]{:S(2)}) copy-start(s32[6144]{0:T(1024)} %param.16) | copy-start | bytes 73732
  143.4 231.5 %all-gather.12.cloned.1.call-start = ((), (), s32[]{:S(2)}) async-start(), calls=%async_computation.5 | async-start | bytes 14155776 | tf_op jit(solution)/shard_map/all_gather | solution.py:47
  144.0 300.1 %all-gather.10.cloned.1.call-start = ((), (), s32[]{:S(2)}) async-start(), calls=%async_computation.4 | async-start | bytes 4325376 | tf_op jit(solution)/shard_map/all_gather | solution.py:45
  246.1 249.9 %all-gather.14.cloned.1.call-start = ((), (), s32[]{:S(2)}) async-start(), calls=%async_computation.6 | async-start | bytes 4718592 | tf_op jit(solution)/shard_map/all_gather | solution.py:60
  246.7 363.3 %reduce-scatter.9.cloned.1.call-start = ((), (), s32[]{:S(2)}) async-start(), calls=%async_computation.8 | async-start | bytes 4325376
  387.5 59.7 %copy-start.8 = (f32[4096]{0:T(1024)S(1)}, f32[4096]{0:T(1024)}, u32[]{:S(2)}) copy-start(f32[4096]{0:T(1024)} %param.14) | copy-start | bytes 49156
  444.0 3.4 copy-start.1
  509.0 0.7 copy-start.9
  509.0 102.0 %copy-start.3 = (bf16[512,128]{1,0:T(8,128)(2,1)S(1)}, bf16[512,128]{1,0:T(8,128)(2,1)}, u32[]{:S(2)}) copy-start(bf16[512,128]{1,0:T(8,128)(2,1)} %add_convert_fusion.1) | copy-start | bytes 393220
  611.0 72.8 %copy-start.5 = (bf16[512,128]{1,0:T(8,128)(2,1)}, bf16[512,128]{1,0:T(8,128)(2,1)S(1)}, u32[]{:S(2)}) copy-start(bf16[512,128]{1,0:T(8,128)(2,1)S(1)} %add_convert_fusion) | copy-start | bytes 393220
Sparse Core Ops, SparseCore 0:
  10.5 67.8 all-gather.5
  80.2 50.1 all-gather.7
  143.5 100.7 reduce-scatter.6
  246.1 128.7 all-gather.11
  378.1 65.8 all-gather.9
  445.8 50.1 all-gather.13
  509.1 100.7 reduce-scatter.8
where the time goes:
time: 691 us
  waiting for transfers between devices  480 us (69%)
  local copies, waits for them, and re-layouts  89 us (13%)
  blocking collectives  72 us (10%)
  matrix products  28.2 us (4%)
  between operations  14.3 us (2%)
  other arithmetic  7.25 us (1%)
    unnamed x9, waiting for transfers between devices  203 us
    all_gather x1, waiting for transfers between devices, shards(): gathered = lax.all_gather(piece_buffer, 'replica', axis=0, tiled=True)  105 us
    psum x1, blocking collectives, shards(): step_logits = lax.psum(local_logits, 'tensor')  72 us
    all_gather x1, waiting for transfers between devices, shards(): full_in = lax.all_gather(tokens, 'tensor', axis=1, tiled=True)  60.3 us
    all_gather x1, waiting for transfers between devices, shards(): lax.all_gather(prev_down, 'replica', axis=1, tiled=True)  41.6 us
    all_gather x1, waiting for transfers between devices, shards(): lax.all_gather(next_down, 'replica', axis=1, tiled=True)  40.5 us
    unnamed x26, local copies, waits for them, and re-layouts  38 us
    all_gather x1, waiting for transfers between devices, shards(): full_mid = lax.all_gather(middle, 'tensor', axis=1, tiled=True)  29.2 us
  transfers between devices with their start and end apart: 7, of which 7 were waited for; matrix products, arithmetic and copies ran while one was open for 14% of the time, Pallas kernels for 0%

commit v1 on v0

v1 whole, which is shorter than its diff:
```python
import jax
import jax.numpy as jnp
from jax import lax
from jax.experimental import pallas as pl
from jax.experimental.pallas import tpu as pltpu
from jax.sharding import PartitionSpec as P

MESH = pl.DeviceIdType.MESH
BF = jnp.bfloat16
F32 = jnp.float32
D = 4096
T = 512
H = T // 2
W = 512
CAP = 768
SLOTS = 8 * CAP
N_SEM = 160
RAW = 256
RAW_SLOTS = 4


def kernel(
    tok_in, gain1, gate_up, down1_in, gain2, piece_in, slots, down2_in, head, pos,
    out, logits,
    act, wprev, raw, down1, down2, pcs, nperm, nbuf, both, hid, sumsq,
    prt, rs_c, y_l, y_r, yt_l, yt_r, z_l, z_r, zt_l, zt_r, lgs,
    ssem, rsem, lsem, raw_sem,
):
    rep = lax.axis_index("replica")
    ten = lax.axis_index("tensor")
    ml, mx = rep // 4, rep % 4
    mz, my, mc = ten // 8, (ten // 2) % 4, ten % 2

    def at(zl=ml, x=mx, z=mz, y=my, c=mc):
        return (zl * 4 + x, (z * 4 + y) * 2 + c)

    def mod4(v):
        return lax.rem(v + 4, 4)

    x_right, x_left = at(x=mod4(mx + 1)), at(x=mod4(mx - 1))
    y_right, y_left = at(y=mod4(my + 1)), at(y=mod4(my - 1))
    z_right, z_left = at(z=mod4(mz + 1)), at(z=mod4(mz - 1))
    sibling = at(c=1 - mc)
    partner = at(zl=1 - ml)

    count = [0]
    unsent = []
    unsent_weights = []

    def send(src, dst, device, pending=unsent):
        i = count[0]
        count[0] += 1
        copy = pltpu.make_async_remote_copy(
            src_ref=src, dst_ref=dst, send_sem=ssem.at[i], recv_sem=rsem.at[i],
            device_id=device, device_id_type=MESH,
        )
        copy.start()
        pending.append(copy)
        return copy

    def drain(pending=unsent):
        for copy in pending:
            copy.wait_send()
        pending.clear()

    def send_weights(src, dst, device):
        return send(src, dst, device, unsent_weights)

    own = act.at[mz, mc, my]
    loads = [
        pltpu.make_async_copy(tok_in, own, lsem.at[0]),
        pltpu.make_async_copy(down1_in, down1.at[rep], lsem.at[1]),
        pltpu.make_async_copy(down2_in, down2.at[rep], lsem.at[2]),
    ]
    for load in loads:
        load.start()

    order = [mz, mod4(mz - 1), mod4(mz + 1), mod4(mz + 2)]
    n_piece = CAP // RAW
    n_raw = n_piece + D // RAW

    def raw_copy(i):
        if i < n_piece:
            src = piece_in.at[pl.ds(i * RAW, RAW)]
        else:
            j = i - n_piece
            src = gate_up.at[pl.ds(pl.multiple_of(order[j // 4] * 1024 + (j % 4) * RAW, RAW), RAW)]
        return pltpu.make_async_copy(src, raw.at[i % RAW_SLOTS], raw_sem.at[i % RAW_SLOTS])

    for i in range(RAW_SLOTS):
        raw_copy(i).start()

    barrier = pltpu.get_barrier_semaphore()
    neighbours = (x_right, x_left, y_right, y_left, z_right, z_left, sibling, partner)
    for n in neighbours:
        pl.semaphore_signal(barrier, inc=1, device_id=n, device_id_type=MESH)

    done = [0]

    def relay(n):
        for _ in range(n):
            i = done[0]
            if i >= n_raw:
                return
            done[0] += 1
            raw_copy(i).wait()
            slot = i % RAW_SLOTS

            def step(k, _):
                rows = pl.ds(pl.multiple_of(k * 64, 64), 64)
                flat = raw[slot, rows].reshape(64, 2 * W)
                if i < n_piece:
                    pcs[rep, pl.ds(pl.multiple_of(i * RAW + k * 64, 64), 64), :] = flat
                else:
                    j = i - n_piece
                    base = order[j // 4] * 1024 + (j % 4) * RAW + k * 64
                    wprev[pl.ds(pl.multiple_of(base, 64), 64), :] = flat
                return 0

            lax.fori_loop(0, RAW // 64, step, 0)
            if i + RAW_SLOTS < n_raw:
                raw_copy(i + RAW_SLOTS).start()

    def gather(buf, half):
        def halves(b):
            return buf.at[b, pl.ds(0, half)], buf.at[b, pl.ds(half, half)]

        left, right, far = mod4(mx - 1), mod4(mx + 1), mod4(mx + 2)
        me = ml * 4
        other = (1 - ml) * 4
        h = {}

        def start():
            b = buf.at[me + mx]
            h["p"] = send_weights(b, b, partner)
            h["r"] = send_weights(b, b, x_right)
            h["l"] = send_weights(b, b, x_left)

        def forward():
            h["r"].wait_recv()
            a, _ = halves(me + left)
            h["ra"] = send_weights(a, a, x_right)
            h["l"].wait_recv()
            _, b = halves(me + right)
            h["lb"] = send_weights(b, b, x_left)

        def relay_partner():
            h["p"].wait_recv()
            b = buf.at[other + mx]
            h["pr"] = send_weights(b, b, x_right)
            h["pl"] = send_weights(b, b, x_left)

        def forward_partner():
            h["pr"].wait_recv()
            a, _ = halves(other + left)
            h["pra"] = send_weights(a, a, x_right)
            h["pl"].wait_recv()
            _, b = halves(other + right)
            h["plb"] = send_weights(b, b, x_left)

        def far_to_partner():
            h["ra"].wait_recv()
            h["lb"].wait_recv()
            b = buf.at[me + far]
            h["pf"] = send_weights(b, b, partner)

        def wait(*names):
            for n in names:
                h[n].wait_recv()

        index = {
            "own": me + mx, "left": me + left, "right": me + right, "far": me + far,
            "pown": other + mx, "pleft": other + left, "pright": other + right, "pfar": other + far,
        }
        return start, forward, relay_partner, forward_partner, far_to_partner, wait, index

    g1 = gather(down1, 256)
    gp = gather(pcs, CAP // 2)
    g2 = gather(down2, 256)

    def blk(q, y=my):
        return act.at[q, mc, y]

    def half_a(ref):
        return ref.at[pl.ds(0, H)]

    def half_b(ref):
        return ref.at[pl.ds(H, H)]

    def activations():
        h = {}
        qz = dict(zip(("own", "left", "right", "far"), order))

        def y_start(k):
            b = blk(qz[k])
            h[k, "r"] = send(b, b, y_right)
            h[k, "l"] = send(b, b, y_left)

        def y_forward(k):
            h[k, "r"].wait_recv()
            a = half_a(blk(qz[k], mod4(my - 1)))
            h[k, "ra"] = send(a, a, y_right)
            h[k, "l"].wait_recv()
            b = half_b(blk(qz[k], mod4(my + 1)))
            h[k, "lb"] = send(b, b, y_left)

        def y_end(k):
            h[k, "ra"].wait_recv()
            h[k, "lb"].wait_recv()
            b = act.at[qz[k], mc]
            h[k, "c"] = send(b, b, sibling)

        def z_start():
            b = blk(mz)
            h["r"] = send(b, b, z_right)
            h["l"] = send(b, b, z_left)

        def z_left_in():
            h["r"].wait_recv()
            a = half_a(blk(qz["left"]))
            h["ra"] = send(a, a, z_right)

        def z_right_in():
            h["l"].wait_recv()
            b = half_b(blk(qz["right"]))
            h["lb"] = send(b, b, z_left)

        def z_end():
            h["ra"].wait_recv()
            h["lb"].wait_recv()

        def whole(k):
            h[k, "c"].wait_recv()

        return y_start, y_forward, y_end, z_start, z_left_in, z_right_in, z_end, whole

    def scaled(q, gain):
        def step(i, _):
            v = act[q, lax.rem(i, 2), i // 2].astype(F32)
            g = gain[pl.ds(q * 8 + i, 1), :]
            nbuf[:, pl.ds(pl.multiple_of(i * 128, 128), 128)] = (v * g).astype(BF)
            sumsq[...] += v * v
            return 0

        lax.fori_loop(0, 8, step, 0)

    def mm_prev(q):
        rows = pl.ds(pl.multiple_of(q * 1024, 1024), 1024)

        def step(j, _):
            cols = pl.ds(pl.multiple_of(j * 256, 256), 256)
            both[:, cols] += jnp.dot(nbuf[...], wprev[rows, cols], preferred_element_type=F32)
            return 0

        lax.fori_loop(0, 4, step, 0)

    def permute(q, first):
        def step(s, _):
            want = slots[pl.ds(s, 1), :] - q * 1024
            rows = lax.broadcasted_iota(jnp.int32, (1024, 256), 0)
            pick = jnp.where(rows == want, 1.0, 0.0).astype(BF)
            moved = jnp.dot(nbuf[...], pick, preferred_element_type=F32)
            if first:
                nperm[s] = moved.astype(BF)
            else:
                nperm[s] = (nperm[s].astype(F32) + moved).astype(BF)
            return 0

        lax.fori_loop(0, SLOTS // 256, step, 0)

    def mm_piece(r):
        def step(j, _):
            cols = pl.ds(pl.multiple_of(j * 256, 256), 256)
            total = both[:, cols]
            for k in range(3):
                total += jnp.dot(
                    nperm[r * 3 + k], pcs[r, pl.ds(k * 256, 256), cols], preferred_element_type=F32
                )
            both[:, cols] = total
            return 0

        lax.fori_loop(0, 4, step, 0)

    def hidden():
        def step(i, _):
            rows = pl.ds(pl.multiple_of(i * 64, 64), 64)
            mean = jnp.sum(sumsq[rows, :], axis=1, keepdims=True) * (1.0 / D)
            scale = lax.rsqrt(mean + 1e-06)
            g = both[rows, pl.ds(0, W)] * scale
            u = both[rows, pl.ds(W, W)] * scale
            hid[rows, :] = (g / (1.0 + jnp.exp(-g)) * u).astype(BF)
            return 0

        lax.fori_loop(0, T // 64, step, 0)

    def reset():
        both[...] = jnp.zeros_like(both)
        sumsq[...] = jnp.zeros_like(sumsq)

    def add(dst, *srcs):
        total = dst[...].astype(F32)
        for s in srcs:
            total += s[...].astype(F32)
        dst[...] = total.astype(BF)

    def reduce(down, ready, extra):
        groups = [mod4(mz + 2), mod4(mz + 1), mod4(mz - 1), mz]
        c_in = {}
        t_in = {}
        y_in = {}
        z_in = {}

        def mult(k):
            q = groups[k]
            ready(k)

            def step(y, _):
                cols = pl.ds(pl.multiple_of(lax.rem(y, 2) * 256, 256), 256)
                term = jnp.dot(hid[...], down[q * 2 + y // 2, :, cols], preferred_element_type=F32)
                prt[q, 0, y] = term[:, :128].astype(BF)
                prt[q, 1, y] = term[:, 128:].astype(BF)
                return 0

            lax.fori_loop(0, 4, step, 0)
            c_in[k] = send(prt.at[q, 1 - mc], rs_c.at[k], sibling)

        def cores(k):
            q = groups[k]
            c_in[k].wait_recv()

            def step(y, _):
                add(prt.at[q, mc, y], rs_c.at[k, y])
                return 0

            lax.fori_loop(0, 4, step, 0)
            far = prt.at[q, mc, mod4(my + 2)]
            t_in[k] = (
                send(half_a(far), yt_l.at[k], y_right),
                send(half_b(far), yt_r.at[k], y_left),
            )

        def y_pass(k):
            q = groups[k]
            t_in[k][0].wait_recv()
            right = prt.at[q, mc, mod4(my + 1)]
            add(half_a(right), yt_l.at[k])
            first = send(right, y_l.at[k], y_right)
            t_in[k][1].wait_recv()
            left = prt.at[q, mc, mod4(my - 1)]
            add(half_b(left), yt_r.at[k])
            second = send(left, y_r.at[k], y_left)
            y_in[k] = (first, second)

        def y_last(k):
            q = groups[k]
            y_in[k][0].wait_recv()
            y_in[k][1].wait_recv()
            mine = prt.at[q, mc, my]
            add(mine, y_l.at[k], y_r.at[k])
            if k == 0:
                z_in["a"] = send(half_a(mine), zt_l, z_right)
                z_in["b"] = send(half_b(mine), zt_r, z_left)
            elif k == 1:
                z_in["a"].wait_recv()
                add(half_a(mine), zt_l)
                z_in["l"] = send(mine, z_l, z_right)
            elif k == 2:
                z_in["b"].wait_recv()
                add(half_b(mine), zt_r)
                z_in["r"] = send(mine, z_r, z_left)
            else:
                z_in["l"].wait_recv()
                z_in["r"].wait_recv()

        mult(0)
        mult(1)
        cores(0)
        mult(2)
        cores(1)
        y_pass(0)
        mult(3)
        cores(2)
        y_pass(1)
        y_last(0)
        cores(3)
        extra(0)
        y_pass(2)
        y_last(1)
        y_pass(3)
        extra(1)
        y_last(2)
        y_last(3)
        total = act[mz, mc, my].astype(F32) + prt[mz, mc, my].astype(F32)
        return (total + z_l[...].astype(F32) + z_r[...].astype(F32)).astype(BF)

    reset()
    pl.semaphore_wait(barrier, len(neighbours))
    loads[0].wait()
    y_start, y_forward, y_end, z_start, z_left_in, z_right_in, z_end, whole = activations()
    z_start()
    y_start("own")
    loads[1].wait()
    g1[0]()
    relay(5)
    z_left_in()
    y_start("left")
    z_right_in()
    y_start("right")
    relay(2)
    y_forward("own")
    relay(2)
    y_forward("left")
    z_end()
    y_start("far")
    g1[1]()
    relay(2)
    y_end("own")
    y_forward("right")
    relay(2)
    g1[2]()
    y_end("left")
    y_forward("far")
    relay(6)
    loads[2].wait()
    whole("own")
    scaled(order[0], gain1)
    mm_prev(order[0])
    y_end("right")
    whole("left")
    scaled(order[1], gain1)
    mm_prev(order[1])
    y_end("far")
    g1[3]()
    gp[0]()
    whole("right")
    scaled(order[2], gain1)
    mm_prev(order[2])
    whole("far")
    scaled(order[3], gain1)
    mm_prev(order[3])
    hidden()
    drain()

    def ready1(k):
        if k == 0:
            g1[5]("ra", "lb", "pra", "plb")

    def extra1(k):
        if k == 0:
            gp[1]()
        if k == 1:
            gp[2]()

    middle = reduce(down1, ready1, extra1)
    own[...] = middle

    reset()
    y_start, y_forward, y_end, z_start, z_left_in, z_right_in, z_end, whole = activations()
    z_start()
    y_start("own")
    g2[0]()
    z_left_in()
    y_start("left")
    z_right_in()
    y_start("right")
    y_forward("own")
    y_forward("left")
    z_end()
    y_start("far")
    y_end("own")
    y_forward("right")
    whole("own")
    scaled(order[0], gain2)
    permute(order[0], True)
    y_end("left")
    y_forward("far")
    gp[4]()
    whole("left")
    scaled(order[1], gain2)
    permute(order[1], False)
    y_end("right")
    whole("right")
    scaled(order[2], gain2)
    permute(order[2], False)
    y_end("far")
    g2[1]()
    whole("far")
    scaled(order[3], gain2)
    permute(order[3], False)
    drain()
    index = gp[6]
    mm_piece(index["own"])
    mm_piece(index["left"])
    mm_piece(index["right"])
    mm_piece(index["far"])
    mm_piece(index["pown"])
    g2[2]()
    gp[5]("pr")
    mm_piece(index["pleft"])
    gp[5]("pl")
    mm_piece(index["pright"])
    gp[5]("pf")
    mm_piece(index["pfar"])
    hidden()
    g2[4]()

    def ready2(k):
        if k == 0:
            g2[5]("pr", "pl", "pf")

    last = reduce(down2, ready2, lambda k: None)
    out[...] = last

    lanes = lax.broadcasted_iota(jnp.int32, (24, T), 1)
    pick = jnp.where(lanes == pos[...], 1.0, 0.0).astype(BF)
    picked = jnp.dot(pick, last, preferred_element_type=F32)
    first = jnp.sum(picked * head[pl.ds(0, 1), :], axis=1, keepdims=True)
    second = jnp.sum(picked * head[pl.ds(1, 1), :], axis=1, keepdims=True)
    lane = lax.broadcasted_iota(jnp.int32, (24, 128), 1)
    lgs[0] = jnp.where(lane == 0, first, jnp.where(lane == 1, second, 0.0))
    a = send(lgs.at[0], lgs.at[1], sibling)
    a.wait_recv()
    lgs[2] = lgs[0] + lgs[1]
    base = 2
    for right, left in ((y_right, y_left), (z_right, z_left)):
        a = send(lgs.at[base], lgs.at[base + 1], right)
        b = send(lgs.at[base], lgs.at[base + 2], left)
        a.wait_recv()
        c = send(lgs.at[base + 1], lgs.at[base + 3], right)
        b.wait_recv()
        c.wait_recv()
        lgs[base + 4] = (lgs[base] + lgs[base + 3]) + (lgs[base + 1] + lgs[base + 2])
        base += 4
    logits[...] = lgs[base][:, :2]
    drain()
    drain(unsent_weights)


def shards(
    tokens, prev_gain, prev_gate_up, prev_down, next_gain, piece_buffer, slot_rows, next_down,
    score_head, step_positions,
):
    hbm = pl.BlockSpec(memory_space=pl.ANY)
    vmem = pl.BlockSpec(memory_space=pltpu.VMEM)
    dma = pltpu.SemaphoreType.DMA
    block = (T, 128)
    return pl.pallas_call(
        kernel,
        out_shape=(
            jax.ShapeDtypeStruct((T, 128), BF),
            jax.ShapeDtypeStruct((24, 2), F32),
        ),
        in_specs=[hbm, vmem, hbm, hbm, vmem, hbm, vmem, hbm, vmem, vmem],
        out_specs=(vmem, vmem),
        scratch_shapes=[
            pltpu.VMEM((4, 2, 4) + block, BF),
            pltpu.VMEM((D, 2 * W), BF),
            pltpu.VMEM((RAW_SLOTS, RAW, 2, W), BF),
            pltpu.VMEM((8, W, 512), BF),
            pltpu.VMEM((8, W, 512), BF),
            pltpu.VMEM((8, CAP, 2 * W), BF),
            pltpu.VMEM((SLOTS // 256, T, 256), BF),
            pltpu.VMEM((T, 1024), BF),
            pltpu.VMEM((T, 2 * W), F32),
            pltpu.VMEM((T, W), BF),
            pltpu.VMEM(block, F32),
            pltpu.VMEM((4, 2, 4) + block, BF),
            pltpu.VMEM((4, 4) + block, BF),
            pltpu.VMEM((4,) + block, BF),
            pltpu.VMEM((4,) + block, BF),
            pltpu.VMEM((4, H, 128), BF),
            pltpu.VMEM((4, H, 128), BF),
            pltpu.VMEM(block, BF),
            pltpu.VMEM(block, BF),
            pltpu.VMEM((H, 128), BF),
            pltpu.VMEM((H, 128), BF),
            pltpu.VMEM((11, 24, 128), F32),
            dma((N_SEM,)),
            dma((N_SEM,)),
            dma((3,)),
            dma((RAW_SLOTS,)),
        ],
        compiler_params=pltpu.CompilerParams(
            collective_id=0, has_side_effects=True, vmem_limit_bytes=62 * 2**20
        ),
        cost_estimate=pl.CostEstimate(
            flops=2 * T * (D * 1024 + SLOTS * 1024 + D * SLOTS + 2 * 512 * D),
            bytes_accessed=16 * 2**20, transcendentals=2 * T * W,
        ),
    )(
        tokens,
        prev_gain.reshape(32, 128),
        prev_gate_up,
        prev_down,
        next_gain.reshape(32, 128),
        piece_buffer,
        slot_rows.reshape(SLOTS // 256, 256),
        next_down,
        score_head.T,
        step_positions.reshape(24, 1),
    )


def solution(mesh):
    in_specs = (
        P("replica", "tensor"),
        P(),
        P(None, None, "tensor"),
        P("tensor", "replica"),
        P(),
        P("replica", None, "tensor"),
        P(),
        P("tensor", "replica"),
        P("tensor", None),
        P("replica"),
    )
    out_specs = (P("replica", "tensor"), P("replica", None))
    return jax.shard_map(shards, mesh=mesh, in_specs=in_specs, out_specs=out_specs, check_vma=False)
```

time: 691 us -> 249 us (0.36)
  waiting for transfers between devices: 480 us -> 0 us
  Pallas kernels: 0 us -> 240 us
  local copies, waits for them, and re-layouts: 89 us -> 5.59 us
  blocking collectives: 72 us -> 0 us
  matrix products: 28.2 us -> 0 us
  between operations: 14.3 us -> 0.64 us
  other arithmetic: 7.25 us -> 0 us
    all_gather x5 -> x0, waiting for transfers between devices: 277 us -> none  [the longest x1 105 us: shards(): gathered = lax.all_gather(piece_buffer, 'replica', axis=0, tiled=True)]
    pallas_call x0 -> x1, Pallas kernels: none -> 240 us  [shards(): pl.pallas_call(kernel, out_shape=(jax.ShapeDtypeStruct((T, 128), BF), jax...]
    unnamed x9 -> x0, waiting for transfers between devices: 203 us -> none
    psum x1 -> x0, blocking collectives: 72 us -> none  [shards(): step_logits = lax.psum(local_logits, 'tensor')]
    unnamed x26 -> x1, local copies, waits for them, and re-layouts: 38 us -> 1.57 us
    dot_general x5 -> x0, matrix products: 28.2 us -> none  [the longest x1 8.01 us: shards(): jnp.dot(normed_next, weights, preferred_element_type=jnp.float32)]
    gather x2 -> x0, local copies, waits for them, and re-layouts: 27.8 us -> none  [the longest x1 27.3 us: shards(): weights = jnp.take(flat_slots, holder, axis=0)]
    scatter x1 -> x0, local copies, waits for them, and re-layouts: 23.2 us -> none  [shards(): holder = jnp.zeros((D + 1,), jnp.int32).at[slot_rows].set(jnp.arange(slot...]
  transfers between devices with their start and end apart: 7 -> 0, of which waited for: 7 -> 0; matrix products, arithmetic and copies ran while one was open for 14% -> 0% of each run, Pallas kernels for 0% -> 0%
where the time goes in v1:
time: 249 us; the launch traced here: 247 us
  Pallas kernels  240 us (96%)
  local copies, waits for them, and re-layouts  5.59 us (2%)
    pallas_call x1, Pallas kernels, shards(): pl.pallas_call(kernel, out_shape=(jax.ShapeDtypeStruct((T, 128), BF), jax...  240 us

profile of v1, /device:TPU:2, one launch (start us, length us, event | category | flops | bytes accessed | tf_op | source)
XLA Modules:
  0.0 246.5 jit_solution(1372448317148102269)
XLA Ops:
  0.6 1.3 copy.12.pos
  2.0 1.4 reshape.18.slots
  3.3 240.3 %shard_map.113 = (bf16[512,128]{1,0:T(8,128)(2,1)}, f32[24,2]{1,0:T(8,128)}) custom-call(bf16[512,128]{1,0:T(8,128)(2,1)} %tok_in.1, f32[32,128]{1,0:T(8,128)} %bitcast.5, bf16[4096,2,512]{2,1,0:T(2,128)(2,1)} %gate_up.1, bf16[512,512]{1,0:T(8,128)(2,1)} %down1_in.1, f32[32,128]{1,0:T(8,128)} %bitcast.6, bf16[768,2,512]{2,1,0:T(2,128)(2,1)} %piece_in.1, ...), custom_call_target="tpu_custom_call" | custom-call | flops 40802189312 | bytes 16777216 | tf_op jit(solution)/shard_map/pallas_call | solution.py:547
  243.6 1.3 copy.13
  245.0 1.6 copy.15

commit v2 on v1

--- a/solution.py
+++ b/solution.py
@@ -11,10 +11,11 @@
 D = 4096
 T = 512
 H = T // 2
+ROWS = T + 16
 W = 512
 CAP = 768
 SLOTS = 8 * CAP
-N_SEM = 160
+N_SEM = 192
 RAW = 256
 RAW_SLOTS = 4
 
@@ -22,7 +23,7 @@
 def kernel(
     tok_in, gain1, gate_up, down1_in, gain2, piece_in, slots, down2_in, head, pos,
     out, logits,
-    act, wprev, raw, down1, down2, pcs, nperm, nbuf, both, hid, sumsq,
+    act, score, wprev, raw, down1, down2, pcs, nperm, rowid, nbuf, both, hid, sumsq,
     prt, rs_c, y_l, y_r, yt_l, yt_r, z_l, z_r, zt_l, zt_r, lgs,
     ssem, rsem, lsem, raw_sem,
 ):
@@ -40,6 +41,7 @@
     x_right, x_left = at(x=mod4(mx + 1)), at(x=mod4(mx - 1))
     y_right, y_left = at(y=mod4(my + 1)), at(y=mod4(my - 1))
     z_right, z_left = at(z=mod4(mz + 1)), at(z=mod4(mz - 1))
+    y_far, z_far = at(y=mod4(my + 2)), at(z=mod4(mz + 2))
     sibling = at(c=1 - mc)
     partner = at(zl=1 - ml)
 
@@ -66,7 +68,7 @@
     def send_weights(src, dst, device):
         return send(src, dst, device, unsent_weights)
 
-    own = act.at[mz, mc, my]
+    own = act.at[mz, mc, my, pl.ds(0, T)]
     loads = [
         pltpu.make_async_copy(tok_in, own, lsem.at[0]),
         pltpu.make_async_copy(down1_in, down1.at[rep], lsem.at[1]),
@@ -90,8 +92,20 @@
     for i in range(RAW_SLOTS):
         raw_copy(i).start()
 
+    row = lax.broadcasted_iota(jnp.int32, (16, 128), 0)
+    terms = jnp.zeros((16, 128), F32)
+    for i in range(2):
+        rest = head[pl.ds(i, 1), :]
+        for j in range(3):
+            part = rest.astype(BF).astype(F32)
+            terms = jnp.where(row == 3 * i + j, part, terms)
+            rest = rest - part
+    act[mz, mc, my, pl.ds(T, 16), :] = terms.astype(BF)
+
     barrier = pltpu.get_barrier_semaphore()
-    neighbours = (x_right, x_left, y_right, y_left, z_right, z_left, sibling, partner)
+    neighbours = (
+        x_right, x_left, y_right, y_left, y_far, z_right, z_left, z_far, sibling, partner,
+    )
     for n in neighbours:
         pl.semaphore_signal(barrier, inc=1, device_id=n, device_id_type=MESH)
 
@@ -121,18 +135,26 @@
             if i + RAW_SLOTS < n_raw:
                 raw_copy(i + RAW_SLOTS).start()
 
-    def gather(buf, half):
+    def gather(buf, first, rows):
+        half = rows // 2
+
+        def whole_of(b):
+            return buf.at[b, pl.ds(first, rows)]
+
         def halves(b):
-            return buf.at[b, pl.ds(0, half)], buf.at[b, pl.ds(half, half)]
+            return buf.at[b, pl.ds(first, half)], buf.at[b, pl.ds(first + half, half)]
 
         left, right, far = mod4(mx - 1), mod4(mx + 1), mod4(mx + 2)
         me = ml * 4
         other = (1 - ml) * 4
         h = {}
 
-        def start():
-            b = buf.at[me + mx]
+        def start_z():
+            b = whole_of(me + mx)
             h["p"] = send_weights(b, b, partner)
+
+        def start_x():
+            b = whole_of(me + mx)
             h["r"] = send_weights(b, b, x_right)
             h["l"] = send_weights(b, b, x_left)
 
@@ -146,11 +168,17 @@
 
         def relay_partner():
             h["p"].wait_recv()
-            b = buf.at[other + mx]
+            b = whole_of(other + mx)
             h["pr"] = send_weights(b, b, x_right)
             h["pl"] = send_weights(b, b, x_left)
 
-        def forward_partner():
+        def far_to_partner():
+            h["ra"].wait_recv()
+            h["lb"].wait_recv()
+            b = whole_of(me + far)
+            h["pf"] = send_weights(b, b, partner)
+
+        def far_by_x():
             h["pr"].wait_recv()
             a, _ = halves(other + left)
             h["pra"] = send_weights(a, a, x_right)
@@ -158,25 +186,18 @@
             _, b = halves(other + right)
             h["plb"] = send_weights(b, b, x_left)
 
-        def far_to_partner():
-            h["ra"].wait_recv()
-            h["lb"].wait_recv()
-            b = buf.at[me + far]
-            h["pf"] = send_weights(b, b, partner)
-
         def wait(*names):
             for n in names:
                 h[n].wait_recv()
 
-        index = {
-            "own": me + mx, "left": me + left, "right": me + right, "far": me + far,
-            "pown": other + mx, "pleft": other + left, "pright": other + right, "pfar": other + far,
+        return {
+            "start_x": start_x, "start_z": start_z, "forward": forward,
+            "partner": relay_partner, "far": far_to_partner, "far_x": far_by_x, "wait": wait,
         }
-        return start, forward, relay_partner, forward_partner, far_to_partner, wait, index
-
-    g1 = gather(down1, 256)
-    gp = gather(pcs, CAP // 2)
-    g2 = gather(down2, 256)
+
+    g1 = gather(down1, 0, W)
+    ga, gb, gc = (gather(pcs, k * 256, 256) for k in range(3))
+    g2 = gather(down2, 0, W)
 
     def blk(q, y=my):
         return act.at[q, mc, y]
@@ -186,6 +207,9 @@
 
     def half_b(ref):
         return ref.at[pl.ds(H, H)]
+
+    def rest_b(ref):
+        return ref.at[pl.ds(H, ROWS - H)]
 
     def activations():
         h = {}
@@ -201,7 +225,7 @@
             a = half_a(blk(qz[k], mod4(my - 1)))
             h[k, "ra"] = send(a, a, y_right)
             h[k, "l"].wait_recv()
-            b = half_b(blk(qz[k], mod4(my + 1)))
+            b = rest_b(blk(qz[k], mod4(my + 1)))
             h[k, "lb"] = send(b, b, y_left)
 
         def y_end(k):
@@ -222,7 +246,7 @@
 
         def z_right_in():
             h["l"].wait_recv()
-            b = half_b(blk(qz["right"]))
+            b = rest_b(blk(qz["right"]))
             h["lb"] = send(b, b, z_left)
 
         def z_end():
@@ -236,7 +260,7 @@
 
     def scaled(q, gain):
         def step(i, _):
-            v = act[q, lax.rem(i, 2), i // 2].astype(F32)
+            v = act[q, lax.rem(i, 2), i // 2, pl.ds(0, T), :].astype(F32)
             g = gain[pl.ds(q * 8 + i, 1), :]
             nbuf[:, pl.ds(pl.multiple_of(i * 128, 128), 128)] = (v * g).astype(BF)
             sumsq[...] += v * v
@@ -255,26 +279,30 @@
         lax.fori_loop(0, 4, step, 0)
 
     def permute(q, first):
-        def step(s, _):
-            want = slots[pl.ds(s, 1), :] - q * 1024
-            rows = lax.broadcasted_iota(jnp.int32, (1024, 256), 0)
-            pick = jnp.where(rows == want, 1.0, 0.0).astype(BF)
-            moved = jnp.dot(nbuf[...], pick, preferred_element_type=F32)
+        def step(i, _):
+            r, k = i // 3 * 2 + mc, lax.rem(i, 3)
+            lanes = pl.ds(pl.multiple_of((r * 3 + k) * 256, 256), 256)
+            want = slots[:, lanes] - q * 1024
+            moved = jnp.zeros((T, 256), F32)
+            for j in range(4):
+                near = (want - j * 256).astype(F32).astype(BF)
+                pick = jnp.where(rowid[...] == near, 1.0, 0.0).astype(BF)
+                moved += jnp.dot(nbuf[:, j * 256 : j * 256 + 256], pick, preferred_element_type=F32)
             if first:
-                nperm[s] = moved.astype(BF)
+                nperm[r, k] = moved.astype(BF)
             else:
-                nperm[s] = (nperm[s].astype(F32) + moved).astype(BF)
+                nperm[r, k] = (nperm[r, k].astype(F32) + moved).astype(BF)
             return 0
 
-        lax.fori_loop(0, SLOTS // 256, step, 0)
-
-    def mm_piece(r):
+        lax.fori_loop(0, SLOTS // 512, step, 0)
+
+    def mm_pieces(k):
         def step(j, _):
             cols = pl.ds(pl.multiple_of(j * 256, 256), 256)
             total = both[:, cols]
-            for k in range(3):
+            for r in range(8):
                 total += jnp.dot(
-                    nperm[r * 3 + k], pcs[r, pl.ds(k * 256, 256), cols], preferred_element_type=F32
+                    nperm[r, k], pcs[r, pl.ds(k * 256, 256), cols], preferred_element_type=F32
                 )
             both[:, cols] = total
             return 0
@@ -389,49 +417,59 @@
         y_pass(3)
         extra(1)
         y_last(2)
+        extra(2)
         y_last(3)
-        total = act[mz, mc, my].astype(F32) + prt[mz, mc, my].astype(F32)
+        total = own[...].astype(F32) + prt[mz, mc, my].astype(F32)
         return (total + z_l[...].astype(F32) + z_r[...].astype(F32)).astype(BF)
 
     reset()
+    rowid[...] = lax.broadcasted_iota(jnp.int32, (256, 256), 0).astype(F32).astype(BF)
     pl.semaphore_wait(barrier, len(neighbours))
     loads[0].wait()
     y_start, y_forward, y_end, z_start, z_left_in, z_right_in, z_end, whole = activations()
     z_start()
     y_start("own")
     loads[1].wait()
-    g1[0]()
-    relay(5)
+    g1["start_x"]()
+    relay(3)
+    ga["start_x"]()
     z_left_in()
     y_start("left")
     z_right_in()
     y_start("right")
-    relay(2)
+    relay(1)
     y_forward("own")
-    relay(2)
+    z_end()
+    g1["start_z"]()
+    y_start("far")
+    relay(1)
     y_forward("left")
-    z_end()
-    y_start("far")
-    g1[1]()
-    relay(2)
+    g1["forward"]()
+    relay(1)
     y_end("own")
     y_forward("right")
-    relay(2)
-    g1[2]()
+    relay(1)
     y_end("left")
+    relay(1)
     y_forward("far")
-    relay(6)
+    relay(1)
+    y_end("right")
+    g1["partner"]()
+    gb["start_x"]()
+    relay(1)
+    y_end("far")
+    g1["far"]()
+    ga["start_z"]()
+    relay(9)
     loads[2].wait()
     whole("own")
     scaled(order[0], gain1)
     mm_prev(order[0])
-    y_end("right")
     whole("left")
     scaled(order[1], gain1)
     mm_prev(order[1])
-    y_end("far")
-    g1[3]()
-    gp[0]()
+    gc["start_x"]()
+    gb["start_z"]()
     whole("right")
     scaled(order[2], gain1)
     mm_prev(order[2])
@@ -443,13 +481,14 @@
 
     def ready1(k):
         if k == 0:
-            g1[5]("ra", "lb", "pra", "plb")
+            g1["wait"]("pr", "pl", "pf")
 
     def extra1(k):
         if k == 0:
-            gp[1]()
+            ga["forward"]()
+            ga["partner"]()
         if k == 1:
-            gp[2]()
+            g2["start_x"]()
 
     middle = reduce(down1, ready1, extra1)
     own[...] = middle
@@ -458,7 +497,6 @@
     y_start, y_forward, y_end, z_start, z_left_in, z_right_in, z_end, whole = activations()
     z_start()
     y_start("own")
-    g2[0]()
     z_left_in()
     y_start("left")
     z_right_in()
@@ -467,71 +505,111 @@
     y_forward("left")
     z_end()
     y_start("far")
+    gc["start_z"]()
+    gb["forward"]()
+    gb["partner"]()
     y_end("own")
     y_forward("right")
+    ga["far"]()
+    y_end("left")
     whole("own")
     scaled(order[0], gain2)
     permute(order[0], True)
-    y_end("left")
     y_forward("far")
-    gp[4]()
+    y_end("right")
+    g2["start_z"]()
+    gc["forward"]()
     whole("left")
     scaled(order[1], gain2)
     permute(order[1], False)
-    y_end("right")
+    y_end("far")
+    gc["partner"]()
+    gb["far"]()
     whole("right")
     scaled(order[2], gain2)
     permute(order[2], False)
-    y_end("far")
-    g2[1]()
+    g2["forward"]()
+    gc["far"]()
     whole("far")
     scaled(order[3], gain2)
     permute(order[3], False)
+    moved = []
+    for i in range(4):
+        part = nperm.at[i * 2 + mc]
+        moved.append(send(part, part, sibling))
+    g2["partner"]()
+    for m in moved:
+        m.wait_recv()
+    for k, g in enumerate((ga, gb, gc)):
+        g["wait"]("pr", "pl", "pf")
+        mm_pieces(k)
+    g2["far_x"]()
+    hidden()
     drain()
-    index = gp[6]
-    mm_piece(index["own"])
-    mm_piece(index["left"])
-    mm_piece(index["right"])
-    mm_piece(index["far"])
-    mm_piece(index["pown"])
-    g2[2]()
-    gp[5]("pr")
-    mm_piece(index["pleft"])
-    gp[5]("pl")
-    mm_piece(index["pright"])
-    gp[5]("pf")
-    mm_piece(index["pfar"])
-    hidden()
-    g2[4]()
 
     def ready2(k):
         if k == 0:
-            g2[5]("pr", "pl", "pf")
-
-    last = reduce(down2, ready2, lambda k: None)
-    out[...] = last
-
-    lanes = lax.broadcasted_iota(jnp.int32, (24, T), 1)
-    pick = jnp.where(lanes == pos[...], 1.0, 0.0).astype(BF)
-    picked = jnp.dot(pick, last, preferred_element_type=F32)
-    first = jnp.sum(picked * head[pl.ds(0, 1), :], axis=1, keepdims=True)
-    second = jnp.sum(picked * head[pl.ds(1, 1), :], axis=1, keepdims=True)
-    lane = lax.broadcasted_iota(jnp.int32, (24, 128), 1)
-    lgs[0] = jnp.where(lane == 0, first, jnp.where(lane == 1, second, 0.0))
-    a = send(lgs.at[0], lgs.at[1], sibling)
-    a.wait_recv()
-    lgs[2] = lgs[0] + lgs[1]
-    base = 2
-    for right, left in ((y_right, y_left), (z_right, z_left)):
-        a = send(lgs.at[base], lgs.at[base + 1], right)
-        b = send(lgs.at[base], lgs.at[base + 2], left)
-        a.wait_recv()
-        c = send(lgs.at[base + 1], lgs.at[base + 3], right)
-        b.wait_recv()
-        c.wait_recv()
+            g2["wait"]("ra", "lb", "pra", "plb")
+
+    logit_in = []
+
+    def total_of(base):
         lgs[base + 4] = (lgs[base] + lgs[base + 3]) + (lgs[base + 1] + lgs[base + 2])
-        base += 4
-    logits[...] = lgs[base][:, :2]
+
+    def exchange(base, right, left, far):
+        for i, device in enumerate((right, left, far)):
+            logit_in.append(send(lgs.at[base], lgs.at[base + 1 + i], device))
+
+    def arrive():
+        for copy in logit_in:
+            copy.wait_recv()
+        logit_in.clear()
+
+    def extra2(k):
+        if k == 0:
+            score[...] = jnp.zeros_like(score)
+
+            def step(r, _):
+                parts = [
+                    act[r // 2, j % 2, lax.rem(r, 2) * 2 + j // 2, pl.ds(T, 16), :] for j in range(4)
+                ]
+                score[...] += lax.dot_general(
+                    down2[r], jnp.concatenate(parts, axis=1), (((1,), (1,)), ((), ())),
+                    preferred_element_type=F32,
+                )
+                return 0
+
+            lax.fori_loop(0, 8, step, 0)
+            rows = lax.broadcasted_iota(jnp.int32, (T, 24), 0)
+            pick = jnp.where(rows == pos[...], 1.0, 0.0).astype(BF)
+            tall = (((0,), (0,)), ((), ()))
+            mids = lax.dot_general(pick, own[...], tall, preferred_element_type=F32)
+            hids = lax.dot_general(pick, hid[...], tall, preferred_element_type=F32)
+            six = jnp.dot(
+                hids, score[...], precision=lax.Precision.HIGHEST, preferred_element_type=F32
+            )
+            lane = lax.broadcasted_iota(jnp.int32, (24, 128), 1)
+            both_logits = jnp.zeros((24, 128), F32)
+            for i in range(2):
+                value = jnp.sum(mids * head[pl.ds(i, 1), :], axis=1, keepdims=True)
+                for j in range(3):
+                    value += six[:, 3 * i + j : 3 * i + j + 1]
+                both_logits = jnp.where(lane == i, value, both_logits)
+            lgs[0] = both_logits
+            logit_in.append(send(lgs.at[0], lgs.at[1], sibling))
+        if k == 1:
+            arrive()
+            lgs[2] = lgs[0] + lgs[1]
+            exchange(2, y_right, y_left, y_far)
+        if k == 2:
+            arrive()
+            total_of(2)
+            exchange(6, z_right, z_left, z_far)
+
+    out[...] = reduce(down2, ready2, extra2)
+    arrive()
+    total_of(6)
+    logits[...] = lgs[10][:, :2]
     drain()
     drain(unsent_weights)
 
@@ -553,13 +631,15 @@
         in_specs=[hbm, vmem, hbm, hbm, vmem, hbm, vmem, hbm, vmem, vmem],
         out_specs=(vmem, vmem),
         scratch_shapes=[
-            pltpu.VMEM((4, 2, 4) + block, BF),
+            pltpu.VMEM((4, 2, 4, ROWS, 128), BF),
+            pltpu.VMEM((W, 16), F32),
             pltpu.VMEM((D, 2 * W), BF),
             pltpu.VMEM((RAW_SLOTS, RAW, 2, W), BF),
             pltpu.VMEM((8, W, 512), BF),
             pltpu.VMEM((8, W, 512), BF),
             pltpu.VMEM((8, CAP, 2 * W), BF),
-            pltpu.VMEM((SLOTS // 256, T, 256), BF),
+            pltpu.VMEM((8, 3, T, 256), BF),
+            pltpu.VMEM((256, 256), BF),
             pltpu.VMEM((T, 1024), BF),
             pltpu.VMEM((T, 2 * W), F32),
             pltpu.VMEM((T, W), BF),
@@ -594,10 +674,10 @@
         prev_down,
         next_gain.reshape(32, 128),
         piece_buffer,
-        slot_rows.reshape(SLOTS // 256, 256),
+        slot_rows.reshape(1, SLOTS),
         next_down,
         score_head.T,
-        step_positions.reshape(24, 1),
+        step_positions.reshape(1, 24),
     )
 
 

time: 249 us -> 199 us (0.80)
  Pallas kernels: 240 us -> 194 us
  local copies, waits for them, and re-layouts: 5.59 us -> 2.91 us
    pallas_call x1, Pallas kernels: 240 us -> 194 us  [shards(): pl.pallas_call(kernel, out_shape=(jax.ShapeDtypeStruct((T, 128), BF), jax...]
    reshape x2 -> x0, local copies, waits for them, and re-layouts: 2.68 us -> none  [the longest x1 1.35 us: shards(): slot_rows.reshape(SLOTS // 256, 256)]
where the time goes in v2:
time: 199 us; the launch traced here: 198 us
  Pallas kernels  194 us (97%)
  local copies, waits for them, and re-layouts  2.91 us (1%)
    pallas_call x1, Pallas kernels, shards(): pl.pallas_call(kernel, out_shape=(jax.ShapeDtypeStruct((T, 128), BF), jax...  194 us

profile of v2, /device:TPU:2, one launch (start us, length us, event | category | flops | bytes accessed | tf_op | source)
XLA Modules:
  0.0 197.6 jit_solution(7365856759603357934)
XLA Ops:
  0.6 194.0 %shard_map.113 = (bf16[512,128]{1,0:T(8,128)(2,1)}, f32[24,2]{1,0:T(8,128)}) custom-call(bf16[512,128]{1,0:T(8,128)(2,1)} %tok_in.1, f32[32,128]{1,0:T(8,128)} %bitcast.6, bf16[4096,2,512]{2,1,0:T(2,128)(2,1)} %gate_up.1, bf16[512,512]{1,0:T(8,128)(2,1)} %down1_in.1, f32[32,128]{1,0:T(8,128)} %bitcast.7, bf16[768,2,512]{2,1,0:T(2,128)(2,1)} %piece_in.1, ...), custom_call_target="tpu_custom_call" | custom-call | flops 40802189312 | bytes 16777216 | tf_op jit(solution)/shard_map/pallas_call | solution.py:625
  194.7 1.3 copy.12
  196.0 1.6 copy.14

commit v3 on v2

--- a/solution.py
+++ b/solution.py
@@ -500,12 +500,12 @@
     z_left_in()
     y_start("left")
     z_right_in()
+    gc["start_z"]()
     y_start("right")
     y_forward("own")
     y_forward("left")
     z_end()
     y_start("far")
-    gc["start_z"]()
     gb["forward"]()
     gb["partner"]()
     y_end("own")

time: 199 us -> 197 us (0.990)
  no operation moved by 1% of the time
where the time goes in v3:
time: 197 us
  Pallas kernels  193 us (98%)
  local copies, waits for them, and re-layouts  2.91 us (1%)
    pallas_call x1, Pallas kernels, shards(): pl.pallas_call(kernel, out_shape=(jax.ShapeDtypeStruct((T, 128), BF), jax...  193 us

profile of v3, /device:TPU:2, one launch (start us, length us, event | category | flops | bytes accessed | tf_op | source)
XLA Modules:
  0.0 196.6 jit_solution(1158865250776736669)
XLA Ops:
  0.6 193.1 %shard_map.113 = (bf16[512,128]{1,0:T(8,128)(2,1)}, f32[24,2]{1,0:T(8,128)}) custom-call(bf16[512,128]{1,0:T(8,128)(2,1)} %tok_in.1, f32[32,128]{1,0:T(8,128)} %bitcast.6, bf16[4096,2,512]{2,1,0:T(2,128)(2,1)} %gate_up.1, bf16[512,512]{1,0:T(8,128)(2,1)} %down1_in.1, f32[32,128]{1,0:T(8,128)} %bitcast.7, bf16[768,2,512]{2,1,0:T(2,128)(2,1)} %piece_in.1, ...), custom_call_target="tpu_custom_call" | custom-call | flops 40802189312 | bytes 16777216 | tf_op jit(solution)/shard_map/pallas_call | solution.py:625
  193.7 1.3 copy.12
  195.0 1.6 copy.14
